TPU v7x, 32 devices: a whole 2x2x4 slice. The times are simulated.
32 devices in a mesh: row: 16 (over z, y, x), col: 2 (over core).
Axes of the slice: x: 2, y: 2, z: 4, core: 2. Of those that a mesh axis runs over, the one named last changes fastest.
Arguments:
- matrix: bfloat16 [6144, 6144], P('row', 'col'), may hold values from -6 to 6
- pattern: int32 [32, 32], P('row', 'col'), may hold values 0 or 1
- inverse: bfloat16 [2, 384, 384], P(None, None, 'col'), may hold values from -0.0625 to 0.0625
Outputs:
- factored: bfloat16 [6144, 6144], P('row', 'col')
All inputs are finite; a program needn't handle non-finite values. No bound on the sum of `pattern` on one device may be relied on, other than what follows from the above.
Results may differ from a plain program's by a relative error of at most 0.0063.
Values may be sent and summed in bfloat16 or wider, within the bound.
A program may use at most 128 MiB of HBM per device.

v0:
```python
import jax
import jax.numpy as jnp
from jax import lax
from jax.sharding import PartitionSpec as P


def broadcast(value, axis, root):
    mine = lax.axis_index(axis) == root
    return lax.psum(jnp.where(mine, value, jnp.zeros_like(value)), axis)


def apply_mask(values, mask):
    rows, cols = values.shape
    mask_rows, mask_cols = mask.shape
    shaped = values.reshape(mask_rows, rows // mask_rows, mask_cols, cols // mask_cols)
    return (shaped * mask[:, None, :, None].astype(values.dtype)).reshape(rows, cols)


def shards(matrix, pattern, inverse):
    local_rows = pattern.shape[0] // 2
    local_cols = pattern.shape[1] // 2
    tile_width = matrix.shape[0] // local_rows
    block_size = tile_width // 2
    n_row = lax.axis_size("row")
    n_col = lax.axis_size("col")
    col_index = lax.axis_index("col")
    row_index = lax.axis_index("row")
    row_tiles_label = jnp.arange(local_rows, dtype=jnp.int32) * n_row + row_index
    col_tiles_label = jnp.arange(local_cols, dtype=jnp.int32) * n_col + col_index
    row_label = jnp.repeat(row_tiles_label, 2)
    col_label = jnp.repeat(col_tiles_label, 2)
    masked = apply_mask(matrix, pattern)
    inverse_full = lax.all_gather(inverse, "col", axis=2, tiled=True)

    def col_tile(values, panel_k):
        spot = panel_k // n_col
        return values[:, spot * tile_width : (spot + 1) * tile_width]

    def col_pattern(panel_k):
        spot = panel_k // n_col
        return pattern[:, 2 * spot : 2 * spot + 2]

    def row_tile(values, panel_k):
        spot = panel_k // n_row
        return values

    def factor_panel(tile, tile_pattern, panel_k):
        keep_mask = tile_pattern * (row_label > panel_k).astype(jnp.int32)[:, None]
        product = jnp.dot(tile, inverse_full[panel_k], preferred_element_type=jnp.float32)
        lower_part = apply_mask(product, keep_mask).astype(jnp.bfloat16)
        return broadcast(lower_part, "col", panel_k % n_col)

    def upper_row(tile, panel_k):
        received = broadcast(tile, "row", panel_k % n_row)
        keep_mask = jnp.broadcast_to(
            (col_label > panel_k).astype(jnp.int32)[None, :], (2, 2 * local_cols)
        )
        return apply_mask(received, keep_mask)

    lower_first = factor_panel(col_tile(masked, 0), col_pattern(0), 0)
    upper_first = upper_row(row_tile(masked, 0), 0)
    running = masked.astype(jnp.float32) - jnp.dot(
        lower_first, upper_first, preferred_element_type=jnp.float32
    )
    current = apply_mask(running, pattern).astype(jnp.bfloat16)
    lower_second = factor_panel(col_tile(current, 1), col_pattern(1), 1)
    upper_second = upper_row(row_tile(current, 1), 1)
    running = running - jnp.dot(lower_second, upper_second, preferred_element_type=jnp.float32)
    rounded = apply_mask(running, pattern).astype(jnp.bfloat16)

    def tile_view(values):
        return values.reshape(2 * local_rows, block_size, local_cols, 2, block_size)

    def spread(lower_part):
        return lower_part.reshape(2 * local_rows, block_size, 1, 2, block_size)

    row_labels_view = row_label[:, None, None, None, None]
    col_labels_view = col_tiles_label[None, None, :, None, None]
    result = tile_view(rounded)
    result = jnp.where((col_labels_view == 1) & (row_labels_view > 1), spread(lower_second), result)
    result = jnp.where((col_labels_view >= 1) & (row_labels_view == 1), tile_view(current), result)
    result = jnp.where((col_labels_view == 0) & (row_labels_view >= 1), spread(lower_first), result)
    result = jnp.where(row_labels_view == 0, tile_view(masked), result)
    return result.reshape(matrix.shape)


def solution(mesh):
    return jax.shard_map(
        shards,
        mesh=mesh,
        in_specs=(P("row", "col"), P("row", "col"), P(None, None, "col")),
        out_specs=P("row", "col"),
        check_vma=False,
    )
```

profile of v0, /device:TPU:24, one launch (start us, length us, event | category | flops | bytes accessed | tf_op | source)
XLA Modules:
  0.0 359.8 jit_solution(10044289058772878099)
XLA Ops:
  6.5 0.8 fusion.15
  7.3 0.3 mul.115
  7.6 4.2 %mul.116 = bf16[384,3072]{1,0:T(8,128)(2,1)} reshape(bf16[2,192,16,192]{3,2,1,0:T(8,128)(2,1)S(1)} %mul.115) | data formatting | bytes 4718592 | tf_op jit(solution)/shard_map/mul | solution.py:16
  11.8 4.1 %broadcast_select_fusion.1 = (bf16[384,3072]{1,0:T(8,128)(2,1)}, bf16[384,3072]{1,0:T(8,128)(2,1)S(1)}) fusion(pred[]{:T(512)S(6)} %eq.32, bf16[384,3072]{1,0:T(8,128)(2,1)} %param.3, bf16[384,3072]{1,0:T(8,128)(2,1)} %mul.116), kind=kLoop, calls=%fused_computation.10 | loop fusion | flops 2359296 | bytes 9437185 | tf_op jit(solution)/shard_map/jit(_where)/select_n | solution.py:9
  15.9 2.2 all_gather.3
  18.3 0.4 fusion.9
  18.7 0.4 copy.4
  19.1 1.0 select_n.53
  20.1 0.7 all-reduce.7.cloned.1.call-update
  20.9 3.5 mul.126
  24.4 7.6 %mul.127 = f32[384,3072]{1,0:T(8,128)} reshape(f32[2,192,16,192]{3,2,1,0:T(8,128)} %mul.126) | data formatting | bytes 9437184 | tf_op jit(solution)/shard_map/mul | solution.py:16
  32.3 7.5 %all-reduce.5.cloned.1.call-done = bf16[384,384]{1,0:T(8,128)(2,1)} async-done(((bf16[384,384]{1,0:T(8,128)(2,1)}), bf16[384,384]{1,0:T(8,128)(2,1)}) %all-reduce.5.cloned.1.call-update) | async-done | bytes 294928 | tf_op jit(solution)/shard_map/psum | solution.py:9
  39.8 136.2 %all-reduce.7.cloned.1.call-done = bf16[384,3072]{1,0:T(8,128)(2,1)} async-done(((bf16[384,3072]{1,0:T(8,128)(2,1)}), bf16[384,3072]{1,0:T(8,128)(2,1)}) %all-reduce.7.cloned.1.call-update) | async-done | bytes 2359312 | tf_op jit(solution)/shard_map/psum | solution.py:9
  176.0 7.6 %broadcast_select_fusion = (bf16[384,3072]{1,0:T(8,128)(2,1)}, bf16[384,3072]{1,0:T(8,128)(2,1)S(1)}, f32[384,3072]{1,0:T(8,128)}) fusion(pred[]{:T(512)S(6)} %eq.35, f32[384,3072]{1,0:T(8,128)} %mul.127, bf16[384,384]{1,0:T(8,128)(2,1)} %all-reduce.5.cloned.1.call-done, bf16[384,3072]{1,0:T(8,128)(2,1)} %all-reduce.7.cloned.1.call-done, ...), kind=kOutput, calls=%fused_computation.9 | convolution fusion | flops 913047552 | bytes 19175424 | tf_op jit(solution)/shard_map/dot_general | solution.py:62
  183.5 1.4 copy-done
  185.0 0.4 fusion.8
  185.4 0.4 copy.5
  185.8 1.0 select_n.57
  186.8 0.2 all-reduce.11.cloned.1.call-start
  187.0 0.3 all-reduce.11.cloned.1.call-update
  187.4 1.7 mul.111
  189.1 4.0 %mul.112 = bf16[384,3072]{1,0:T(8,128)(2,1)} reshape(bf16[2,192,8,2,192]{4,3,2,1,0:T(2,128)(2,1)S(1)} %mul.111) | data formatting | bytes 4718592 | tf_op jit(solution)/shard_map/mul | solution.py:16
  193.6 0.7 broadcast_in_dim.80
  194.6 1.2 broadcast_in_dim.82
  195.8 1.6 broadcast_in_dim.83
  197.4 4.0 %broadcast_in_dim.84 = bf16[384,3072]{1,0:T(8,128)(2,1)} reshape(bf16[2,192,8,2,192]{4,3,2,1,0:T(2,128)(2,1)S(1)} %broadcast_in_dim.83) | data formatting | bytes 4718592 | tf_op jit(solution)/shard_map/jit(_where)/broadcast_in_dim | solution.py:82
  201.4 5.0 %all-reduce.9.cloned.1.call-done = bf16[384,384]{1,0:T(8,128)(2,1)} async-done(((bf16[384,384]{1,0:T(8,128)(2,1)}), bf16[384,384]{1,0:T(8,128)(2,1)}) %all-reduce.9.cloned.1.call-update) | async-done | bytes 294928 | tf_op jit(solution)/shard_map/psum | solution.py:9
  206.4 1.2 broadcast_in_dim.92
  207.6 1.6 broadcast_in_dim.93
  209.3 4.0 %broadcast_in_dim.94 = bf16[384,3072]{1,0:T(8,128)(2,1)} reshape(bf16[2,192,8,2,192]{4,3,2,1,0:T(2,128)(2,1)S(1)} %broadcast_in_dim.93) | data formatting | bytes 4718592 | tf_op jit(solution)/shard_map/jit(_where)/broadcast_in_dim | solution.py:80
  213.3 130.0 %all-reduce.11.cloned.1.call-done = bf16[384,3072]{1,0:T(8,128)(2,1)} async-done(((bf16[384,3072]{1,0:T(8,128)(2,1)}), bf16[384,3072]{1,0:T(8,128)(2,1)}) %all-reduce.11.cloned.1.call-update) | async-done | bytes 2359312 | tf_op jit(solution)/shard_map/psum | solution.py:9
  343.3 10.0 %fusion.3 = bf16[384,3072]{1,0:T(8,128)(2,1)} fusion(bf16[384,3072]{1,0:T(8,128)(2,1)} %broadcast_in_dim.84, bf16[384,3072]{1,0:T(8,128)(2,1)} %copy-done, bf16[384,3072]{1,0:T(8,128)(2,1)} %broadcast_in_dim.94, f32[384,3072]{1,0:T(8,128)} %mul.127, f32[384,3072]{1,0:T(8,128)} %get-tuple-element.15, bf16[384,384]{1,0:T(8,128)(2,1)S(1)} %copy-done.1, ...), kind=kOutput, calls=%fused_computation.6 | convolution fusion | flops 916586496 | bytes 26262528 | tf_op jit(solution)/shard_map/dot_general | solution.py:68
  (35 shorter events, 1.4 us)
Async XLA Ops:
  6.5 33.3 %all-reduce.5.cloned.1.call-start = ((), (), s32[]{:S(2)}) async-start(), calls=%async_computation | async-start | bytes 589824 | tf_op jit(solution)/shard_map/psum | solution.py:9
  11.8 4.2 %copy-start.2 = (bf16[2,384,192]{1,2,0:T(8,128)(2,1)S(1)}, bf16[2,384,192]{1,2,0:T(8,128)(2,1)}, u32[]{:S(2)}) copy-start(bf16[2,384,192]{1,2,0:T(8,128)(2,1)} %param.5) | copy-start | bytes 884740
  15.9 2.4 copy-start.4
  20.1 155.9 %all-reduce.7.cloned.1.call-start = ((), (), s32[]{:S(2)}) async-start(), calls=%async_computation.1 | async-start | bytes 4718592 | tf_op jit(solution)/shard_map/psum | solution.py:9
  20.8 185.6 %all-reduce.9.cloned.1.call-start = ((), (), s32[]{:S(2)}) async-start(), calls=%async_computation.2 | async-start | bytes 589824 | tf_op jit(solution)/shard_map/psum | solution.py:9
  183.5 1.4 copy-start
  186.8 156.6 %all-reduce.11.cloned.1.call-start = ((), (), s32[]{:S(2)}) async-start(), calls=%async_computation.3 | async-start | bytes 4718592 | tf_op jit(solution)/shard_map/psum | solution.py:9
  209.3 134.1 %copy-start.1 = (bf16[384,384]{1,0:T(8,128)(2,1)S(1)}, bf16[384,384]{1,0:T(8,128)(2,1)}, u32[]{:S(2)}) copy-start(bf16[384,384]{1,0:T(8,128)(2,1)} %all-reduce.9.cloned.1.call-done) | copy-start | bytes 884740
  209.3 134.0 %copy-start.3 = (pred[3072]{0:T(1024)(128)(4,1)S(1)}, pred[3072]{0:T(1024)(128)(4,1)}, u32[]{:S(2)}) copy-start(pred[3072]{0:T(1024)(128)(4,1)} %broadcast_in_dim.80) | copy-start | bytes 9220
Sparse Core Ops, SparseCore 0:
  20.2 19.5 all-reduce.4
  45.4 130.5 all-reduce.6
  186.9 19.4 all-reduce.8
  212.8 130.4 all-reduce.10
where the time goes:
time: 363 us; the launch traced here: 360 us
  waiting for transfers between devices  280 us (77%)
  local copies, waits for them, and re-layouts  41.1 us (11%)
  matrix products  18.3 us (5%)
  between operations  13.3 us (4%)
  other arithmetic  4.92 us (1%)
    psum x4, waiting for transfers between devices, broadcast(): return lax.psum(jnp.where(mine, value, jnp.zeros_like(value)), axis)  279 us
    mul x11, local copies, waits for them, and re-layouts, apply_mask(): shaped * mask[:, None, :, None].astype(values.dtype)  21.7 us
    dot_general x1, matrix products, shards(): jnp.dot(lower_second, upper_second, preferred_element_type=jnp.float32)  9.97 us
    broadcast_in_dim x5, local copies, waits for them, and re-layouts, shards(): jnp.where((col_labels_view == 0) & (row_labels_view >= 1), spread(lower_f...  7.59 us
    dot_general x1, matrix products, shards(): jnp.dot(lower_first, upper_first, preferred_element_type=jnp.float32)  7.57 us
  transfers between devices with their start and end apart: 4, of which 4 were waited for; matrix products, arithmetic and copies ran while one was open for 9% of the time, Pallas kernels for 0%

commit v1 on v0

v1 whole, which is shorter than its diff:
```python
import functools

import jax
import jax.numpy as jnp
from jax import lax
from jax.experimental import pallas as pl
from jax.experimental.pallas import tpu as pltpu
from jax.sharding import PartitionSpec as P

TREES = 3
SPLIT = 2
LANES = 128
STRIP = 16
MESH = pl.DeviceIdType.MESH
BF16 = jnp.bfloat16
F32 = jnp.float32

PARENTS_16 = (
    (None, 0, 0, 2, 6, 7, 2, 6, 10, 11, 6, 10, 14, 15, 10, 14),
    (None, 3, 0, 2, 0, 4, 4, 3, 4, 8, 8, 10, 8, 12, 10, 14),
    (None, 0, 6, 7, 0, 4, 4, 6, 4, 8, 6, 9, 8, 12, 12, 13),
)


def grid_of(n_row):
    if n_row == 16:
        return (4, 2, 2)
    if n_row % 4 == 0 and n_row > 4:
        return (4, n_row // 4)
    return (n_row,)


def ordered_parents(n_row, root, order):
    dims = grid_of(n_row)
    strides = [1] * len(dims)
    for i in range(len(dims) - 2, -1, -1):
        strides[i] = strides[i + 1] * dims[i + 1]
    parents = [None] * n_row
    for r in range(n_row):
        for i in order:
            here, there = (r // strides[i]) % dims[i], (root // strides[i]) % dims[i]
            if here != there:
                parents[r] = r + (strides[i] if there > here else -strides[i])
                break
    return parents


def all_trees(n_row):
    if n_row == 16:
        first = [list(p) for p in PARENTS_16]
        second = [[None if p[r ^ 1] is None else p[r ^ 1] ^ 1 for r in range(16)] for p in first]
        return first + second
    axes = list(range(len(grid_of(n_row))))
    orders = [axes if t % 2 == 0 else axes[::-1] for t in range(TREES)]
    return [ordered_parents(n_row, root, order) for root in (0, 1) for order in orders]


def pack_tree(parents):
    n_row = len(parents)
    packed, depths = [], []
    for r in range(n_row):
        depth, at = 0, r
        while parents[at] is not None:
            depth, at = depth + 1, parents[at]
        children = [c for c in range(n_row) if parents[c] == r]
        assert len(children) <= 3 and n_row <= 64 and depth < 32
        padded = children + [r] * (3 - len(children))
        packed.append(depth + 32 * (len(children) + 4 * (padded[0] + 64 * (padded[1] + 64 * padded[2]))))
        depths.append(depth)
    return packed, max(depths)


def select(values, index):
    out = jnp.int32(values[0])
    for i in range(1, len(values)):
        out = jnp.where(index == i, jnp.int32(values[i]), out)
    return out


def kernel(
    n_row, n_col, width, m_ref, pat_ref, inv_ref, out_ref,
    ua, ub, mask, l1, l11, l2, invb,
    recv_sem, send_sem, x_recv, x_send, inv_recv, inv_send, own_sem,
):
    row, col = lax.axis_index("row"), lax.axis_index("col")
    rows, cols = m_ref.shape
    half = rows // 2
    slabs = cols // LANES
    per_tile = width // LANES
    tiles = cols // width
    steps = slabs // TREES * SPLIT

    barrier = pltpu.get_barrier_semaphore()
    dims = grid_of(n_row)
    expected = jnp.int32(n_col - 1)
    stride = n_row
    for size in dims:
        stride = stride // size
        place = (row // stride) % size
        for ok, other in ((place > 0, row - stride), (place < size - 1, row + stride)):
            expected = expected + ok.astype(jnp.int32)

            @pl.when(ok)
            def _(other=other):
                pl.semaphore_signal(barrier, inc=1, device_id={"row": other}, device_id_type=MESH)

    for c in range(n_col):
        @pl.when(col != c)
        def _(c=c):
            pl.semaphore_signal(barrier, inc=1, device_id={"col": jnp.int32(c)}, device_id_type=MESH)

    wide = (pat_ref.shape[1], cols)
    block = cols // pat_ref.shape[1]
    lane = lax.broadcasted_iota(jnp.int32, wide, 1)
    first = lax.broadcasted_iota(jnp.int32, wide, 0) * block
    spread = jnp.where((lane >= first) & (lane < first + block), 1.0, 0.0).astype(BF16)
    mask[...] = jnp.dot(pat_ref[...].astype(F32).astype(BF16), spread, preferred_element_type=F32)

    def source(dst, strip):
        for s in range(slabs):
            at = slice(s * LANES, (s + 1) * LANES)
            for h in range(2):
                keep = mask[h:h + 1, at]
                dst[s, h, 0:half, :] = (m_ref[h * half:(h + 1) * half, at].astype(F32) * keep).astype(BF16)
                if strip:
                    dst[s, h, half:half + STRIP, :] = jnp.broadcast_to(keep, (STRIP, LANES)).astype(BF16)

    @pl.when(row == 0)
    def _():
        source(ua, False)

    @pl.when(row == 1)
    def _():
        source(ub, True)

    pl.semaphore_wait(barrier, expected)

    shard = inv_ref.shape[1]
    for k in range(2):
        mine = invb.at[pl.ds(pl.multiple_of(col * shard, 16), shard)]

        @pl.when(col != k)
        def _(k=k, mine=mine):
            pltpu.make_async_remote_copy(
                inv_ref.at[k], mine, inv_send.at[k], inv_recv.at[col],
                device_id={"col": jnp.int32(k)}, device_id_type=MESH,
            ).start()

        @pl.when(col == k)
        def _(k=k, mine=mine):
            pltpu.make_async_copy(inv_ref.at[k], mine, own_sem).start()

    def wait_inverse():
        pltpu.make_async_copy(
            inv_ref.at[0], invb.at[pl.ds(pl.multiple_of(col * shard, 16), shard)], own_sem
        ).wait()
        for c in range(n_col):
            @pl.when(col != c)
            def _(c=c):
                pltpu.make_async_remote_copy(
                    inv_ref.at[0], invb.at[pl.ds(c * shard, shard)], inv_send.at[0], inv_recv.at[c],
                    device_id={"col": jnp.int32(c)}, device_id_type=MESH,
                ).wait_recv()

    def to_columns(buffer, which, root, act):
        for c in range(n_col):
            if c != root:
                act(pltpu.make_async_remote_copy(
                    buffer, buffer, x_send.at[which, c], x_recv.at[which],
                    device_id={"col": jnp.int32(c)}, device_id_type=MESH,
                ))

    def from_column(buffer, which, root):
        @pl.when(col != root)
        def _():
            pltpu.make_async_remote_copy(
                buffer, buffer, x_send.at[which, root], x_recv.at[which],
                device_id={"col": jnp.int32(root)}, device_id_type=MESH,
            ).wait_recv()

    def tile_of(ref, j):
        halves = [
            jnp.concatenate([ref[per_tile * j + i, h, 0:half, :] for i in range(per_tile)], axis=1)
            for h in range(2)
        ]
        return jnp.concatenate(halves, axis=0)

    def two(top, bottom):
        return jnp.concatenate(
            [jnp.broadcast_to(top, (half, width)), jnp.broadcast_to(bottom, (half, width))], axis=0
        )

    def columns(j):
        return pl.ds(pl.multiple_of(j * width, width), width)

    def mask_of(j):
        keep = mask[:, columns(j)]
        return two(keep[0:1], keep[1:2])

    def upper_mask(j):
        strips = [
            jnp.concatenate(
                [ub[per_tile * j + i, h, half:half + STRIP, :].astype(F32)[0:1] for i in range(per_tile)], axis=1
            )
            for h in range(2)
        ]
        return two(*strips)

    def dot(a, b):
        return jnp.dot(a, b, preferred_element_type=F32)

    def dot_t(a, b):
        return lax.dot_general(a, b, (((1,), (1,)), ((), ())), preferred_element_type=F32)

    def make_l1():
        @pl.when(col < 2)
        def _():
            wait_inverse()

        @pl.when(col == 0)
        def _():
            keep = mask_of(0)
            tile = (m_ref[:, 0:width].astype(F32) * keep).astype(BF16)
            alive = (row > 0).astype(F32)
            l1[...] = (dot_t(tile, invb[...]) * (keep * alive)).astype(BF16)
            to_columns(l1, 0, 0, lambda copy: copy.start())

    def make_l2():
        @pl.when(col == 0)
        def _():
            l11[...] = (dot_t(tile_of(ub, 0), invb[...]) * upper_mask(0)).astype(BF16)
            to_columns(l11, 1, 0, lambda copy: copy.start())

        from_column(l1, 0, 0)

        @pl.when(col == 1)
        def _():
            keep = mask_of(0)
            one = ((m_ref[:, 0:width].astype(F32) - dot(l1[...], tile_of(ua, 0))) * keep).astype(BF16)
            alive = (row > 1).astype(F32)
            l2[...] = (dot_t(one, invb[...]) * (keep * alive)).astype(BF16)
            to_columns(l2, 2, 1, lambda copy: copy.start())

    def update(j):
        upper = tile_of(ua, j)
        row_one = ((tile_of(ub, j).astype(F32) - dot(l11[...], upper)) * upper_mask(j)).astype(BF16)
        total = m_ref[:, columns(j)].astype(F32) - dot(l1[...], upper) - dot(l2[...], row_one)
        out_ref[:, columns(j)] = (total * mask_of(j)).astype(BF16)

    plans, deepest = [], 0
    for t, parents in enumerate(all_trees(n_row)):
        packed, depth = pack_tree(parents)
        deepest = max(deepest, depth)
        code = select(packed, row)
        depth, code = code % 32, code // 32
        count, code = code % 4, code // 4
        plans.append((t, depth, count, (code % 64, (code // 64) % 64, code // 4096)))

    def chunk(t, k):
        buffer = ua if t < TREES else ub
        slab = TREES * (k // SPLIT) + t % TREES
        return buffer.at[slab] if SPLIT == 1 else buffer.at[slab, k % SPLIT]

    def tree_copy(t, k, j, target):
        return pltpu.make_async_remote_copy(
            chunk(t, k), chunk(t, k), send_sem.at[t, j], recv_sem.at[t, k],
            device_id={"row": target}, device_id_type=MESH,
        )

    @pl.loop(0, steps + deepest + 1)
    def _(now):
        for i in range(2 * TREES):
            t, depth, count, children = plans[(i % 2) * TREES + i // 2]
            k = now - depth

            @pl.when((k >= 0) & (k < steps))
            def _(t=t, depth=depth, count=count, children=children, k=k):
                @pl.when(depth > 0)
                def _():
                    tree_copy(t, k, 0, children[0]).wait_recv()

                for j in range(3):
                    @pl.when(count > j)
                    def _(j=j):
                        tree_copy(t, k, j, children[j]).start()

        @pl.when(now == 1)
        def _():
            make_l1()

        done = now - (SPLIT + deepest)

        @pl.when(done == -1)
        def _():
            make_l2()

        @pl.when(done == 0)
        def _():
            from_column(l11, 1, 0)
            from_column(l2, 2, 1)

        @pl.when((done >= 0) & (done % SPLIT == 0))
        def _():
            update(done // SPLIT)

    @pl.when((col == 0) & (row >= 1))
    def _():
        out_ref[:, 0:width] = l1[...]

    @pl.when((col == 1) & (row >= 2))
    def _():
        out_ref[:, 0:width] = l2[...]

    for t, depth, count, children in plans:
        buffer = ua if t < TREES else ub
        whole = buffer.at[0:slabs // TREES]
        for j in range(3):
            @pl.when(count > j)
            def _(t=t, j=j, whole=whole, children=children):
                pltpu.make_async_remote_copy(
                    whole, whole, send_sem.at[t, j], recv_sem.at[t, 0],
                    device_id={"row": children[j]}, device_id_type=MESH,
                ).wait_send()

    for k in range(2):
        @pl.when(col != k)
        def _(k=k):
            pltpu.make_async_remote_copy(
                inv_ref.at[k], invb.at[0:shard], inv_send.at[k], inv_recv.at[0],
                device_id={"col": jnp.int32(k)}, device_id_type=MESH,
            ).wait_send()

    @pl.when(col == 0)
    def _():
        to_columns(l1, 0, 0, lambda copy: copy.wait_send())
        to_columns(l11, 1, 0, lambda copy: copy.wait_send())

    @pl.when(col == 1)
    def _():
        to_columns(l2, 2, 1, lambda copy: copy.wait_send())


def solution(mesh):
    n_row, n_col = mesh.shape["row"], mesh.shape["col"]

    def shards(matrix, pattern, inverse):
        rows, cols = matrix.shape
        width = inverse.shape[1]
        half = rows // 2
        slabs = cols // LANES
        steps = slabs // TREES * SPLIT
        turned = jnp.swapaxes(inverse, 1, 2)
        flops = 2 * rows * cols * width * 3
        return pl.pallas_call(
            functools.partial(kernel, n_row, n_col, width),
            out_shape=jax.ShapeDtypeStruct(matrix.shape, BF16),
            in_specs=[pl.BlockSpec(memory_space=pltpu.VMEM)] * 3,
            out_specs=pl.BlockSpec(memory_space=pltpu.VMEM),
            scratch_shapes=[
                pltpu.VMEM((slabs, 2, half, LANES), BF16),
                pltpu.VMEM((slabs, 2, half + STRIP, LANES), BF16),
                pltpu.VMEM((2, cols), F32),
                pltpu.VMEM((rows, width), BF16),
                pltpu.VMEM((width, width), BF16),
                pltpu.VMEM((rows, width), BF16),
                pltpu.VMEM((width, width), BF16),
                pltpu.SemaphoreType.DMA((2 * TREES, steps)),
                pltpu.SemaphoreType.DMA((2 * TREES, 3)),
                pltpu.SemaphoreType.DMA((3,)),
                pltpu.SemaphoreType.DMA((3, n_col)),
                pltpu.SemaphoreType.DMA((n_col,)),
                pltpu.SemaphoreType.DMA((2,)),
                pltpu.SemaphoreType.DMA,
            ],
            compiler_params=pltpu.CompilerParams(
                collective_id=0, has_side_effects=True, vmem_limit_bytes=48 * 1024 * 1024
            ),
            cost_estimate=pl.CostEstimate(flops=flops, bytes_accessed=4 * rows * cols, transcendentals=0),
        )(matrix, pattern, turned)

    return jax.shard_map(
        shards,
        mesh=mesh,
        in_specs=(P("row", "col"), P("row", "col"), P(None, None, "col")),
        out_specs=P("row", "col"),
        check_vma=False,
    )
```

time: 363 us -> 75.4 us (0.21)
  waiting for transfers between devices: 280 us -> 0 us
  Pallas kernels: 0 us -> 70.3 us
  local copies, waits for them, and re-layouts: 41.1 us -> 4.71 us
  matrix products: 18.3 us -> 0 us
  between operations: 13.3 us -> 0.01 us
  other arithmetic: 4.92 us -> 0 us
    psum x4 -> x0, waiting for transfers between devices: 279 us -> none  [broadcast(): return lax.psum(jnp.where(mine, value, jnp.zeros_like(value)), axis)]
    pallas_call x0 -> x1, Pallas kernels: none -> 70.3 us  [shards(): pl.pallas_call(functools.partial(kernel, n_row, n_col, width), out_shape=...]
    mul x11 -> x0, local copies, waits for them, and re-layouts: 21.7 us -> none  [apply_mask(): shaped * mask[:, None, :, None].astype(values.dtype)]
    dot_general x4 -> x0, matrix products: 18.3 us -> none  [the longest x1 9.97 us: shards(): jnp.dot(lower_second, upper_second, preferred_element_type=jnp.float32)]
    broadcast_in_dim x14 -> x0, local copies, waits for them, and re-layouts: 14.9 us -> none  [the longest x5 7.59 us: shards(): jnp.where((col_labels_view == 0) & (row_labels_view >= 1), spread(lower_f...]
    select_n x1 -> x0, other arithmetic: 4.13 us -> none  [broadcast(): return lax.psum(jnp.where(mine, value, jnp.zeros_like(value)), axis)]
  transfers between devices with their start and end apart: 4 -> 0, of which waited for: 4 -> 0; matrix products, arithmetic and copies ran while one was open for 9% -> 0% of each run, Pallas kernels for 0% -> 0%
where the time goes in v1:
time: 75.4 us; the launch traced here: 75.1 us
  Pallas kernels  70.3 us (93%)
  local copies, waits for them, and re-layouts  4.71 us (6%)
    pallas_call x1, Pallas kernels, shards(): pl.pallas_call(functools.partial(kernel, n_row, n_col, width), out_shape=...  70.3 us
    unnamed x7, local copies, waits for them, and re-layouts  4.71 us

profile of v1, /device:TPU:24, one launch (start us, length us, event | category | flops | bytes accessed | tf_op | source)
XLA Modules:
  0.0 75.1 jit_solution(7084712361364617399)
XLA Ops:
  0.0 0.0 copy-start
  0.0 1.7 %copy-done = bf16[384,3072]{1,0:T(8,128)(2,1)S(1)} copy-done((bf16[384,3072]{1,0:T(8,128)(2,1)S(1)}, bf16[384,3072]{1,0:T(8,128)(2,1)}, u32[]{:S(2)}) %copy-start) | copy-done | bytes 2359320
  1.7 0.0 copy-start.1
  1.7 1.0 %copy-done.1 = bf16[2,384,192]{1,2,0:T(8,128)(2,1)S(1)} copy-done((bf16[2,384,192]{1,2,0:T(8,128)(2,1)S(1)}, bf16[2,384,192]{1,2,0:T(8,128)(2,1)}, u32[]{:S(2)}) %copy-start.1) | copy-done | bytes 294936
  2.6 0.0 copy-start.2
  2.6 0.7 copy-done.2
  3.3 70.3 %shard_map.37 = bf16[384,3072]{1,0:T(8,128)(2,1)S(1)} custom-call(bf16[384,3072]{1,0:T(8,128)(2,1)S(1)} %copy-done, s32[2,16]{1,0:T(2,128)S(1)} %copy-done.2, bf16[2,192,384]{2,1,0:T(8,128)(2,1)S(1)} %bitcast.1), custom_call_target="tpu_custom_call" | custom-call | flops 2717908992 | bytes 4718592 | tf_op jit(solution)/shard_map/pallas_call | solution.py:354
  73.7 1.4 %copy.5 = bf16[384,3072]{1,0:T(8,128)(2,1)} copy(bf16[384,3072]{1,0:T(8,128)(2,1)S(1)} %shard_map.37) | data formatting | bytes 4718592
Async XLA Ops:
  0.0 1.7 %copy-start = (bf16[384,3072]{1,0:T(8,128)(2,1)S(1)}, bf16[384,3072]{1,0:T(8,128)(2,1)}, u32[]{:S(2)}) copy-start(bf16[384,3072]{1,0:T(8,128)(2,1)} %m_ref.1) | copy-start | bytes 7077892
  1.7 1.0 %copy-start.1 = (bf16[2,384,192]{1,2,0:T(8,128)(2,1)S(1)}, bf16[2,384,192]{1,2,0:T(8,128)(2,1)}, u32[]{:S(2)}) copy-start(bf16[2,384,192]{1,2,0:T(8,128)(2,1)} %param.5) | copy-start | bytes 884740
  2.6 0.7 copy-start.2

commit v2 on v1

--- a/solution.py
+++ b/solution.py
@@ -8,7 +8,8 @@
 from jax.sharding import PartitionSpec as P
 
 TREES = 3
-SPLIT = 2
+SPLIT = 4
+LAG = 4
 LANES = 128
 STRIP = 16
 MESH = pl.DeviceIdType.MESH
@@ -78,17 +79,26 @@
 
 
 def kernel(
-    n_row, n_col, width, m_ref, pat_ref, inv_ref, out_ref,
-    ua, ub, mask, l1, l11, l2, invb,
-    recv_sem, send_sem, x_recv, x_send, inv_recv, inv_send, own_sem,
+    n_row, n_col, width, m_hbm, pat_hbm, inv_ref, out_ref,
+    m_ref, pat_ref, ua, ub, mask, umask, strip, l1, l11, l2, invb,
+    recv_sem, send_sem, strip_recv, strip_send, x_recv, x_send, inv_recv, inv_send, own_sem, in_sem,
 ):
     row, col = lax.axis_index("row"), lax.axis_index("col")
     rows, cols = m_ref.shape
     half = rows // 2
+    part = rows // SPLIT
     slabs = cols // LANES
     per_tile = width // LANES
-    tiles = cols // width
     steps = slabs // TREES * SPLIT
+
+    def load(i):
+        at = pl.ds(0, width) if i == 0 else pl.ds(width, cols - width)
+        return pltpu.make_async_copy(m_hbm.at[:, at], m_ref.at[:, at], in_sem.at[i])
+
+    pattern_load = pltpu.make_async_copy(pat_hbm, pat_ref, in_sem.at[2])
+    pattern_load.start()
+    load(0).start()
+    load(1).start()
 
     barrier = pltpu.get_barrier_semaphore()
     dims = grid_of(n_row)
@@ -109,30 +119,52 @@
         def _(c=c):
             pl.semaphore_signal(barrier, inc=1, device_id={"col": jnp.int32(c)}, device_id_type=MESH)
 
-    wide = (pat_ref.shape[1], cols)
-    block = cols // pat_ref.shape[1]
-    lane = lax.broadcasted_iota(jnp.int32, wide, 1)
-    first = lax.broadcasted_iota(jnp.int32, wide, 0) * block
-    spread = jnp.where((lane >= first) & (lane < first + block), 1.0, 0.0).astype(BF16)
-    mask[...] = jnp.dot(pat_ref[...].astype(F32).astype(BF16), spread, preferred_element_type=F32)
-
-    def source(dst, strip):
-        for s in range(slabs):
-            at = slice(s * LANES, (s + 1) * LANES)
-            for h in range(2):
-                keep = mask[h:h + 1, at]
-                dst[s, h, 0:half, :] = (m_ref[h * half:(h + 1) * half, at].astype(F32) * keep).astype(BF16)
-                if strip:
-                    dst[s, h, half:half + STRIP, :] = jnp.broadcast_to(keep, (STRIP, LANES)).astype(BF16)
-
-    @pl.when(row == 0)
-    def _():
-        source(ua, False)
+    blocks = pat_ref.shape[1]
+
+    def iota(shape, axis):
+        return lax.broadcasted_iota(jnp.int32, shape, axis)
+
+    def ones_where(condition):
+        return jnp.where(condition, 1.0, 0.0).astype(BF16)
+
+    def expand(tile):
+        lane = iota((LANES, cols), 1)
+        first = iota((LANES, cols), 0) * (cols // blocks)
+        return jnp.dot(
+            tile, ones_where((lane >= first) & (lane < first + cols // blocks)), preferred_element_type=F32
+        )[0:2]
+
+    pattern_load.wait()
+    padded = jnp.dot(
+        pat_ref[...].astype(F32).astype(BF16),
+        ones_where(iota((blocks, LANES), 0) == iota((blocks, LANES), 1)),
+        preferred_element_type=F32,
+    ).astype(BF16)
+    own = jnp.dot(
+        ones_where(iota((STRIP, 2), 0) == iota((STRIP, 2), 1)), padded, preferred_element_type=F32
+    ).astype(BF16)
+    mask[...] = expand(own)
 
     @pl.when(row == 1)
     def _():
-        source(ub, True)
-
+        strip[...] = own
+
+    for skip, buffer in ((0, ua), (1, ub)):
+        @pl.when((col == skip) & (row != skip))
+        def _(buffer=buffer):
+            buffer[0:per_tile] = jnp.zeros((per_tile, SPLIT, part, LANES), BF16)
+
+    def source(dst, k):
+        tile, sub = k // SPLIT, k % SPLIT
+        at = pl.ds(pl.multiple_of(tile * width, width), width)
+        keep = mask[:, at]
+        keep = jnp.where(sub >= SPLIT // 2, keep[1:2], keep[0:1])
+        values = m_ref[pl.ds(pl.multiple_of(sub * part, part), part), at].astype(F32)
+        values = (values * keep).astype(BF16)
+        for i in range(per_tile):
+            dst[per_tile * tile + i, sub, :, :] = values[:, i * LANES:(i + 1) * LANES]
+
+    load(0).wait()
     pl.semaphore_wait(barrier, expected)
 
     shard = inv_ref.shape[1]
@@ -179,11 +211,11 @@
             ).wait_recv()
 
     def tile_of(ref, j):
-        halves = [
-            jnp.concatenate([ref[per_tile * j + i, h, 0:half, :] for i in range(per_tile)], axis=1)
-            for h in range(2)
+        parts = [
+            jnp.concatenate([ref[per_tile * j + i, p, :, :] for i in range(per_tile)], axis=1)
+            for p in range(SPLIT)
         ]
-        return jnp.concatenate(halves, axis=0)
+        return jnp.concatenate(parts, axis=0)
 
     def two(top, bottom):
         return jnp.concatenate(
@@ -193,18 +225,12 @@
     def columns(j):
         return pl.ds(pl.multiple_of(j * width, width), width)
 
-    def mask_of(j):
-        keep = mask[:, columns(j)]
+    def mask_of(j, ref=mask):
+        keep = ref[:, columns(j)]
         return two(keep[0:1], keep[1:2])
 
     def upper_mask(j):
-        strips = [
-            jnp.concatenate(
-                [ub[per_tile * j + i, h, half:half + STRIP, :].astype(F32)[0:1] for i in range(per_tile)], axis=1
-            )
-            for h in range(2)
-        ]
-        return two(*strips)
+        return mask_of(j, umask)
 
     def dot(a, b):
         return jnp.dot(a, b, preferred_element_type=F32)
@@ -226,6 +252,8 @@
             to_columns(l1, 0, 0, lambda copy: copy.start())
 
     def make_l2():
+        umask[...] = expand(strip[...])
+
         @pl.when(col == 0)
         def _():
             l11[...] = (dot_t(tile_of(ub, 0), invb[...]) * upper_mask(0)).astype(BF16)
@@ -250,7 +278,7 @@
     plans, deepest = [], 0
     for t, parents in enumerate(all_trees(n_row)):
         packed, depth = pack_tree(parents)
-        deepest = max(deepest, depth)
+        deepest = max(deepest, LAG * depth)
         code = select(packed, row)
         depth, code = code % 32, code // 32
         count, code = code % 4, code // 4
@@ -258,8 +286,7 @@
 
     def chunk(t, k):
         buffer = ua if t < TREES else ub
-        slab = TREES * (k // SPLIT) + t % TREES
-        return buffer.at[slab] if SPLIT == 1 else buffer.at[slab, k % SPLIT]
+        return buffer.at[TREES * (k // SPLIT) + t % TREES, k % SPLIT]
 
     def tree_copy(t, k, j, target):
         return pltpu.make_async_remote_copy(
@@ -267,13 +294,38 @@
             device_id={"row": target}, device_id_type=MESH,
         )
 
+    def strip_copy(j, target):
+        return pltpu.make_async_remote_copy(
+            strip, strip, strip_send.at[j], strip_recv, device_id={"row": target}, device_id_type=MESH,
+        )
+
+    def skipped(t):
+        return col == t // TREES
+
     @pl.loop(0, steps + deepest + 1)
     def _(now):
+        for r, buffer in ((0, ua), (1, ub)):
+            @pl.when((row == r) & (now < steps))
+            def _(buffer=buffer):
+                source(buffer, now)
+
         for i in range(2 * TREES):
             t, depth, count, children = plans[(i % 2) * TREES + i // 2]
-            k = now - depth
-
-            @pl.when((k >= 0) & (k < steps))
+            k = now - LAG * depth
+
+            if t == TREES:
+                @pl.when(k == 0)
+                def _(depth=depth, count=count, children=children):
+                    @pl.when(depth > 0)
+                    def _():
+                        strip_copy(0, children[0]).wait_recv()
+
+                    for j in range(3):
+                        @pl.when(count > j)
+                        def _(j=j):
+                            strip_copy(j, children[j]).start()
+
+            @pl.when((k >= jnp.where(skipped(t), SPLIT, 0)) & (k < steps))
             def _(t=t, depth=depth, count=count, children=children, k=k):
                 @pl.when(depth > 0)
                 def _():
@@ -286,6 +338,7 @@
 
         @pl.when(now == 1)
         def _():
+            load(1).wait()
             make_l1()
 
         done = now - (SPLIT + deepest)
@@ -313,14 +366,26 @@
 
     for t, depth, count, children in plans:
         buffer = ua if t < TREES else ub
-        whole = buffer.at[0:slabs // TREES]
+        each = slabs // TREES
         for j in range(3):
-            @pl.when(count > j)
-            def _(t=t, j=j, whole=whole, children=children):
+            def left(n, t=t, j=j, buffer=buffer, children=children):
                 pltpu.make_async_remote_copy(
-                    whole, whole, send_sem.at[t, j], recv_sem.at[t, 0],
+                    buffer.at[0:n], buffer.at[0:n], send_sem.at[t, j], recv_sem.at[t, 0],
                     device_id={"row": children[j]}, device_id_type=MESH,
                 ).wait_send()
+
+            @pl.when((count > j) & skipped(t))
+            def _(left=left):
+                left(each - 1)
+
+            @pl.when((count > j) & jnp.logical_not(skipped(t)))
+            def _(left=left):
+                left(each)
+
+            if t == TREES:
+                @pl.when(count > j)
+                def _(j=j, children=children):
+                    strip_copy(j, children[j]).wait_send()
 
     for k in range(2):
         @pl.when(col != k)
@@ -346,7 +411,6 @@
     def shards(matrix, pattern, inverse):
         rows, cols = matrix.shape
         width = inverse.shape[1]
-        half = rows // 2
         slabs = cols // LANES
         steps = slabs // TREES * SPLIT
         turned = jnp.swapaxes(inverse, 1, 2)
@@ -354,26 +418,33 @@
         return pl.pallas_call(
             functools.partial(kernel, n_row, n_col, width),
             out_shape=jax.ShapeDtypeStruct(matrix.shape, BF16),
-            in_specs=[pl.BlockSpec(memory_space=pltpu.VMEM)] * 3,
+            in_specs=[pl.BlockSpec(memory_space=pltpu.HBM)] * 3,
             out_specs=pl.BlockSpec(memory_space=pltpu.VMEM),
             scratch_shapes=[
-                pltpu.VMEM((slabs, 2, half, LANES), BF16),
-                pltpu.VMEM((slabs, 2, half + STRIP, LANES), BF16),
+                pltpu.VMEM((rows, cols), BF16),
+                pltpu.VMEM(pattern.shape, jnp.int32),
+                pltpu.VMEM((slabs, SPLIT, rows // SPLIT, LANES), BF16),
+                pltpu.VMEM((slabs, SPLIT, rows // SPLIT, LANES), BF16),
                 pltpu.VMEM((2, cols), F32),
+                pltpu.VMEM((2, cols), F32),
+                pltpu.VMEM((STRIP, LANES), BF16),
                 pltpu.VMEM((rows, width), BF16),
                 pltpu.VMEM((width, width), BF16),
                 pltpu.VMEM((rows, width), BF16),
                 pltpu.VMEM((width, width), BF16),
                 pltpu.SemaphoreType.DMA((2 * TREES, steps)),
                 pltpu.SemaphoreType.DMA((2 * TREES, 3)),
+                pltpu.SemaphoreType.DMA,
+                pltpu.SemaphoreType.DMA((3,)),
                 pltpu.SemaphoreType.DMA((3,)),
                 pltpu.SemaphoreType.DMA((3, n_col)),
                 pltpu.SemaphoreType.DMA((n_col,)),
                 pltpu.SemaphoreType.DMA((2,)),
                 pltpu.SemaphoreType.DMA,
+                pltpu.SemaphoreType.DMA((3,)),
             ],
             compiler_params=pltpu.CompilerParams(
-                collective_id=0, has_side_effects=True, vmem_limit_bytes=48 * 1024 * 1024
+                collective_id=0, has_side_effects=True, vmem_limit_bytes=62 * 1024 * 1024
             ),
             cost_estimate=pl.CostEstimate(flops=flops, bytes_accessed=4 * rows * cols, transcendentals=0),
         )(matrix, pattern, turned)

time: 75.4 us -> 58.7 us (0.78)
  Pallas kernels: 70.3 us -> 55.3 us
  local copies, waits for them, and re-layouts: 4.71 us -> 3.22 us
    pallas_call x1, Pallas kernels: 70.3 us -> 55.3 us  [shards(): pl.pallas_call(functools.partial(kernel, n_row, n_col, width), out_shape=...]
    unnamed x7 -> x1, local copies, waits for them, and re-layouts: 4.71 us -> 3.22 us
where the time goes in v2:
time: 58.7 us; the launch traced here: 58.5 us
  Pallas kernels  55.3 us (94%)
  local copies, waits for them, and re-layouts  3.22 us (5%)
    pallas_call x1, Pallas kernels, shards(): pl.pallas_call(functools.partial(kernel, n_row, n_col, width), out_shape=...  55.3 us
    unnamed x1, local copies, waits for them, and re-layouts  3.22 us

profile of v2, /device:TPU:24, one launch (start us, length us, event | category | flops | bytes accessed | tf_op | source)
XLA Modules:
  0.0 58.5 jit_solution(784162476938069592)
XLA Ops:
  0.0 55.3 %shard_map.37 = bf16[384,3072]{1,0:T(8,128)(2,1)} custom-call(bf16[384,3072]{1,0:T(8,128)(2,1)} %m_hbm.1, s32[2,16]{1,0:T(2,128)} %pat_hbm.1, bf16[2,192,384]{2,1,0:T(8,128)(2,1)} %bitcast.1), custom_call_target="tpu_custom_call" | custom-call | flops 2717908992 | bytes 4718592 | tf_op jit(solution)/shard_map/pallas_call | solution.py:418
  55.3 3.2 %copy.5 = bf16[384,3072]{1,0:T(8,128)(2,1)} copy(bf16[384,3072]{1,0:T(8,128)(2,1)} %shard_map.37) | data formatting | bytes 4718592
